TPU v7x, 128 devices: a whole 4x4x4 slice. The times are simulated.
128 devices in a mesh: pipe: 2 (over core), dp: 32 (over x_hi, z, y), seq: 2 (over x_lo).
Axes of the slice: x: 4 (x_hi: 2, x_lo: 2; x = x_hi * 2 + x_lo), y: 4, z: 4, core: 2. Of those that a mesh axis runs over, the one named last changes fastest.
Arguments:
- activations: float32 [4, 32768, 256], P(None, ('dp', 'seq')), may hold values from -6 to 6
- cotangent: float32 [4, 32768, 256], P(None, ('dp', 'seq')), may hold values from -6 to 6
- cell_lengths: int32 [4, 32, 3], P(None, 'dp'), may hold values from 0 to 1023, as said below
- w_qkv: float32 [2, 256, 768], P('pipe'), may hold values from -0.375 to 0.375
- b_qv: float32 [2, 512], P('pipe'), may hold values from -3 to 3
- w_out: float32 [2, 256, 256], P('pipe'), may hold values from -1.5 to 1.5
- b_out: float32 [2, 256], P('pipe'), may hold values from -3 to 3
- gain_one: float32 [2, 256], P('pipe'), may hold values from 0.5 to 1.5
- shift_one: float32 [2, 256], P('pipe'), may hold values from -3 to 3
- w_in: float32 [2, 256, 512], P('pipe'), may hold values from -0.375 to 0.375
- b_in: float32 [2, 512], P('pipe'), may hold values from -3 to 3
- w_back: float32 [2, 512, 256], P('pipe'), may hold values from -0.25 to 0.25
- b_back: float32 [2, 256], P('pipe'), may hold values from -3 to 3
- gain_two: float32 [2, 256], P('pipe'), may hold values from 0.5 to 1.5
- shift_two: float32 [2, 256], P('pipe'), may hold values from -3 to 3
Outputs:
- final_output: float32 [4, 32768, 256], P('pipe', ('dp', 'seq'))
- input_grad: float32 [4, 32768, 256], P('pipe', ('dp', 'seq'))
- grad_w_qkv: float32 [2, 256, 768], P('pipe')
- grad_b_qv: float32 [2, 512], P('pipe')
- grad_w_out: float32 [2, 256, 256], P('pipe')
- grad_b_out: float32 [2, 256], P('pipe')
- grad_gain_one: float32 [2, 256], P('pipe')
- grad_shift_one: float32 [2, 256], P('pipe')
- grad_w_in: float32 [2, 256, 512], P('pipe')
- grad_b_in: float32 [2, 512], P('pipe')
- grad_w_back: float32 [2, 512, 256], P('pipe')
- grad_b_back: float32 [2, 256], P('pipe')
- grad_gain_two: float32 [2, 256], P('pipe')
- grad_shift_two: float32 [2, 256], P('pipe')
Inputs may be any that keep to these rules, and one draw needn't show every extreme that they name: cell_lengths[m, g] lists three cells packed from the start of group g's slot of micro-batch m: the first has 1 to 256 tokens, the last 0 to 256, the middle one the rest, and the middle one always covers place 512 of the slot. Together they fill 512 + 512 // 8 to 1024 places. In every micro-batch one group fills exactly 1024 places with a middle cell of 1023 tokens and an empty last cell.
All inputs are finite; a program needn't handle non-finite values.
Results may differ from a plain program's by a relative error of at most 0.0003.
Values sent between devices are 32-bit elements; how exact they have to be, the bound alone decides.
A program may use at most 256 MiB of HBM per device.

v0:
```python
import math

import jax
import jax.numpy as jnp
from jax import lax
from jax.experimental import pallas as pl
from jax.experimental.pallas import tpu as pltpu
from jax.sharding import PartitionSpec as P

MESH = pl.DeviceIdType.MESH
F32 = jnp.float32
BF16 = jnp.bfloat16

HEADS = 4
HEAD = 64
WIDTH = 256
INNER = 512
HALF = 512
SLOT = 1024
BLOCK = 256
BLOCKS = SLOT // BLOCK
DEEP = 3 * HEAD + 16
EPSILON = 1e-06
APART = -1e30
LOG2E = math.log2(math.e)
LN2 = math.log(2.0)
QUERY_SCALE = LOG2E / math.sqrt(HEAD)
KEY_SCALE = 1.0 / math.sqrt(HEAD)

UNITS, UNIT_ROWS, UNIT_HALF = 4, 1024, 512
CHUNKS = (128, 32, 8)
SMALL_ROWS = 16
VMEM_BYTES = 64 * 2 ** 20 - 2 ** 18
V_Q, V_V, V_OUT, V_GAIN1, V_SHIFT1, V_IN, V_BACK, V_GAIN2, V_SHIFT2 = 0, 1, 2, 3, 4, 5, 7, 8, 9


def dot(left, right, left_t=False, right_t=False):
    dims = (((0 if left_t else 1,), (1 if right_t else 0,)), ((), ()))
    return lax.dot_general(left, right, dims, preferred_element_type=F32)


def split(values):
    high = values.astype(BF16)
    return high, (values - high.astype(F32)).astype(BF16)


def dot3(left_high, left_low, right_high, right_low, left_t=False, right_t=False):
    return (
        dot(left_high, right_high, left_t, right_t)
        + dot(left_high, right_low, left_t, right_t)
        + dot(left_low, right_high, left_t, right_t)
    )


def skewed(tasks):
    waiting, running = list(tasks), []
    while waiting or running:
        if waiting:
            running.insert(0, waiting.pop(0))
        for task in list(running):
            if next(task, "end") == "end":
                running.remove(task)


def staged(count, first, second, third):
    first(0)
    for index in range(count + 1):
        if index + 1 < count:
            first(index + 1)
        if index > 0:
            third(index - 1)
        if index < count:
            second(index)


def col_mean(values):
    return jnp.mean(values, axis=0, keepdims=True)


def norm_rows(values):
    center = values - col_mean(values)
    spread = col_mean(center * center)
    inverse = lax.rsqrt(spread + EPSILON)
    return center * inverse, inverse


def norm_back(grad, normed, inverse):
    return (grad - col_mean(grad) - normed * col_mean(grad * normed)) * inverse


def feature_tile(base, values, first):
    high = values.astype(BF16).astype(F32)
    rest = values - high
    middle = rest.astype(BF16).astype(F32)
    low = rest - middle
    row = lax.broadcasted_iota(jnp.int32, base.shape, 0)
    tile = jnp.where(row == first, high, base)
    tile = jnp.where(row == first + 1, middle, tile)
    return jnp.where(row == first + 2, low, tile).astype(BF16)


def lane_fold(values):
    folded = values[:, :128]
    for first in range(128, values.shape[1], 128):
        folded = folded + values[:, first:first + 128]
    return folded


class Torus:
    def __init__(self):
        self.core = lax.axis_index("pipe")
        self.half = lax.axis_index("seq")
        dp = lax.axis_index("dp")
        x_high, z, y = dp // 16, (dp // 4) % 4, dp % 4
        self.sibling = {"pipe": 1 - self.core}
        self.partner = {"seq": 1 - self.half}
        self.axes = {
            "x": (x_high * 2 + self.half, lambda i: {"dp": (i // 2) * 16 + dp % 16, "seq": i % 2}),
            "y": (y, lambda i: {"dp": dp - y + i}),
            "z": (z, lambda i: {"dp": x_high * 16 + i * 4 + y}),
        }

        self.far_x = [{"dp": (1 - x_high) * 16 + dp % 16, "seq": i} for i in range(2)]
        self.near = {
            axis: [((index + step) % 4, where((index + step) % 4)) for step in (1, 2, 3)]
            for axis, (index, where) in self.axes.items()
        }

    def peer(self, axis, step):
        return self.near[axis][step - 1]

    def peers(self, axis):
        return self.near[axis]


class Sender:
    def __init__(self, send_sem, recv_sem):
        self.send_sem, self.recv_sem, self.used = send_sem, recv_sem, 0

    def take(self):
        self.used += 1
        return self.used - 1

    def __call__(self, src, dst, device):
        return self.build(self.take(), src, dst, device)

    def build(self, index, src, dst, device):
        return pltpu.make_async_remote_copy(
            src_ref=src, dst_ref=dst, send_sem=self.send_sem.at[index], recv_sem=self.recv_sem.at[index],
            device_id=device, device_id_type=MESH,
        )


def span(first, size):
    return pl.ds(pl.multiple_of(first, size), size)


class UnitSum:
    def __init__(self, torus, remote, bufs, total_ref, local_sems, layer, first, count, order):
        self.torus, self.remote, self.bufs = torus, remote, bufs
        self.total_ref, self.local_sems = total_ref, local_sems
        self.layer, self.units, self.order = layer, slice(first, first + count), order
        self.pending = []
        self.next = 0

    def send(self, makers):
        self.pending = [(self.remote.take(), maker) for maker in makers]
        for index, maker in self.pending:
            self.remote.build(index, *maker()).start()

    def settle(self):
        for index, maker in self.pending:
            self.remote.build(index, *maker()).wait()
        self.pending = []

    def offset(self, depth):
        first = 0
        for level in range(depth):
            first = first + self.torus.axes[self.order[level]][0] * CHUNKS[level]
        return first

    def step(self):
        getattr(self, "step_%d" % self.next)()
        self.next += 1

    def step_0(self):
        self.send([lambda: (
            self.bufs["grads"].at[self.layer, self.units, span((1 - self.torus.core) * UNIT_HALF, UNIT_HALF)],
            self.bufs["cores"].at[self.layer, self.units], self.torus.sibling)])

    def base(self, level):
        return self.torus.core * UNIT_HALF if level == 0 else 0

    def scatter(self, level, source):
        size = CHUNKS[level]
        slots = self.bufs["slots"][level]

        def maker(step):
            def make():
                peer, device = self.torus.peer(self.order[level], step)
                return (source.at[self.layer, self.units, span(self.base(level) + peer * size, size)],
                        slots.at[step - 1, self.layer, self.units], device)
            return make

        self.send([maker(step) for step in (1, 2, 3)])

    def gathered(self, level, source):
        size = CHUNKS[level]
        slots = self.bufs["slots"][level]
        first = self.base(level) + self.torus.axes[self.order[level]][0] * size
        own = source[self.layer, self.units, span(first, size), :]
        return (own + slots[0, self.layer, self.units]) + (
            slots[1, self.layer, self.units] + slots[2, self.layer, self.units])

    def step_1(self):
        self.settle()
        grads, cores = self.bufs["grads"], self.bufs["cores"]
        home = span(self.torus.core * UNIT_HALF, UNIT_HALF)
        grads[self.layer, self.units, home, :] += cores[self.layer, self.units]
        self.scatter(0, grads)

    def step_2(self):
        self.settle()
        partial = self.bufs["partial"][0]
        partial[self.layer, self.units] = self.gathered(0, self.bufs["grads"])
        self.scatter(1, partial)

    def step_3(self):
        self.settle()
        partial = self.bufs["partial"][1]
        partial[self.layer, self.units] = self.gathered(1, self.bufs["partial"][0])
        self.scatter(2, partial)

    def spread(self, level):
        size = CHUNKS[level]

        def maker(step):
            def make():
                chunk = self.bufs["done"].at[self.layer, self.units, span(self.offset(level + 1), size)]
                return chunk, chunk, self.torus.peer(self.order[level], step)[1]
            return make

        self.send([maker(step) for step in (1, 2, 3)])

    def step_4(self):
        self.settle()
        rows = span(self.offset(3), CHUNKS[2])
        self.bufs["done"][self.layer, self.units, rows, :] = self.gathered(2, self.bufs["partial"][1])
        self.spread(2)

    def step_5(self):
        self.settle()
        self.spread(1)

    def step_6(self):
        self.settle()
        self.spread(0)

    def away_copy(self):
        return self.remote.build(
            self.away, self.bufs["done"].at[self.layer, self.units], self.bufs["far"].at[self.units], self.torus.sibling)

    def near_copy(self):
        return pltpu.make_async_copy(
            self.bufs["done"].at[self.layer, self.units],
            self.total_ref.at[self.units, span(self.torus.core * UNIT_HALF, UNIT_HALF)], self.local_sems.at[0])

    def far_copy(self):
        return pltpu.make_async_copy(
            self.bufs["far"].at[self.units],
            self.total_ref.at[self.units, span((1 - self.torus.core) * UNIT_HALF, UNIT_HALF)], self.local_sems.at[1])

    def step_7(self):
        self.settle()
        self.away = self.remote.take()

        @pl.when(self.torus.core == self.layer)
        def _():
            self.near_copy().start()

        @pl.when(self.torus.core != self.layer)
        def _():
            self.away_copy().start()

    def step_8(self):
        @pl.when(self.torus.core == self.layer)
        def _():
            self.away_copy().wait_recv()
            self.far_copy().start()
            self.near_copy().wait()
            self.far_copy().wait()

        @pl.when(self.torus.core != self.layer)
        def _():
            self.away_copy().wait_send()


def relay_kernel(
    act_ref, cot_ref, len_ref, w_qkv_ref, w_out_ref, w_in_ref, w_back_ref,
    b_qv_ref, b_out_ref, gain_one_ref, shift_one_ref, b_in_ref, b_back_ref, gain_two_ref, shift_two_ref,
    final_ref, grad_ref, total_ref, small_ref,
    x_in, lengths, vecs, p_qkv, p_out, p_in, p_back, cols,
    marks, live, x_now, x_parts, q_all, k_all, v_all, ctx_parts,
    n_one, r_one, slope, inner_parts, n_two, r_two,
    dl_parts, du_parts, do_all, dkv, dqkv, sums,
    grads, cores, slots_0, slots_1, slots_2, partial_0, partial_1, done, far, small, small_far, small_slots,
    local_sem, out_sem, send_sem, recv_sem,
):
    torus = Torus()
    core, half = torus.core, torus.half
    remote = Sender(send_sem, recv_sem)

    barrier = pltpu.get_barrier_semaphore()
    pl.semaphore_signal(barrier, inc=1, device_id=torus.partner, device_id_type=MESH)
    pl.semaphore_signal(barrier, inc=1, device_id=torus.sibling, device_id_type=MESH)
    for axis in "yz":
        for _, device in torus.peers(axis):
            pl.semaphore_signal(barrier, inc=1, device_id=device, device_id_type=MESH)
    pl.semaphore_signal(barrier, inc=1, device_id=torus.far_x[0], device_id_type=MESH)
    pl.semaphore_signal(barrier, inc=1, device_id=torus.far_x[1], device_id_type=MESH)

    mine = 2 * core + half
    theirs = 2 * core + 1 - half

    def weight_pairs(layer):
        return (
            (w_qkv_ref.at[0], slope.at[layer, 0:WIDTH, 0:768]),
            (w_out_ref.at[0], slope.at[layer, WIDTH:INNER, 0:WIDTH]),
            (w_in_ref.at[0], slope.at[layer, WIDTH:INNER, WIDTH:768]),
            (w_back_ref.at[0], slope.at[layer, 0:INNER, 768:SLOT]),
        )

    len_own = pltpu.make_async_copy(len_ref, lengths, local_sem.at[0])
    x_own = pltpu.make_async_copy(act_ref.at[mine], x_in.at[0], local_sem.at[1])
    c_owns = [
        pltpu.make_async_copy(cot_ref.at[mine, :, pl.ds(part * 128, 128)], far.at[part], local_sem.at[9 + part])
        for part in range(2)
    ]
    w_owns = [
        pltpu.make_async_copy(src, dst, local_sem.at[3 + i])
        for i, (src, dst) in enumerate(weight_pairs(core))
    ]
    len_own.start()
    x_own.start()
    for copy in w_owns:
        copy.start()
    vecs[core] = jnp.concatenate([
        b_qv_ref[:, :WIDTH], b_qv_ref[:, WIDTH:], b_out_ref[...], gain_one_ref[...], shift_one_ref[...],
        b_in_ref[:, :WIDTH], b_in_ref[:, WIDTH:], b_back_ref[...], gain_two_ref[...], shift_two_ref[...],
        jnp.zeros((6, WIDTH), F32)], axis=0)

    pl.semaphore_wait(barrier, 10)

    x_sends = [
        remote(act_ref.at[theirs, pl.ds(part * BLOCK, BLOCK)], x_in.at[1, pl.ds(part * BLOCK, BLOCK)], torus.partner)
        for part in range(2)
    ]
    c_sends = [
        remote(cot_ref.at[theirs, :, pl.ds(part * 128, 128)], far.at[2 + part], torus.partner) for part in range(2)
    ]
    w_sends = [remote(src, dst, torus.sibling) for src, dst in weight_pairs(core)]
    w_sends.append(remote(vecs.at[core], vecs.at[core], torus.sibling))
    for copy in x_sends + w_sends:
        copy.start()
    for copy in c_owns:
        copy.start()

    len_own.wait()
    lane = lax.broadcasted_iota(jnp.int32, (16, SLOT), 1)
    row = lax.broadcasted_iota(jnp.int32, (16, SLOT), 0)
    place = jnp.where(lane < HALF, half * HALF + lane, (1 - half) * HALF + lane - HALF)
    end_0 = lengths[0, 0, mine]
    end_1 = end_0 + lengths[1, 0, mine]
    end_2 = end_1 + lengths[2, 0, mine]
    one = jnp.ones_like(place)
    none = jnp.zeros_like(place)
    cell = (
        jnp.where(place >= end_0, one, none)
        + jnp.where(place >= end_1, one, none)
        + jnp.where(place >= end_2, one, none)
    )
    same = jnp.where(cell == row, 1.0, 0.0)
    marks[...] = same
    live[...] = jnp.where(cell < 3, 1.0, 0.0)[:8]
    key_marks = jnp.where(row < 4, (1.0 - same) * APART, jnp.where(row < 7, 1.0, 0.0)).astype(BF16)
    value_marks = jnp.where(row < 3, 1.0, 0.0).astype(BF16)
    query_marks = same.astype(BF16)
    for layer in range(2):
        for head in range(HEADS):
            q_all[layer, head, 192:208, :] = query_marks
            k_all[layer, head, 192:208, :] = key_marks
            v_all[layer, head, 192:208, :] = value_marks

    def load_weights(layer):
        cols[layer] = jnp.concatenate([vecs[layer].T, jnp.zeros((WIDTH, 128 - SMALL_ROWS), F32)], axis=1)
        p_qkv[layer, 0], p_qkv[layer, 1] = split(slope[layer, 0:WIDTH, 0:768])
        p_out[layer, 0], p_out[layer, 1] = split(slope[layer, WIDTH:INNER, 0:WIDTH])
        p_in[layer, 0], p_in[layer, 1] = split(slope[layer, WIDTH:INNER, WIDTH:768])
        p_back[layer, 0], p_back[layer, 1] = split(slope[layer, 0:INNER, 768:SLOT])

    def col(layer, index):
        return cols[layer, :, index:index + 1]

    def block_at(block):
        return slice(block * BLOCK, (block + 1) * BLOCK)

    def project_block(layer, block):
        at = block_at(block)
        x_high, x_low = split(x_now[:, at])
        x_parts[layer, 0, :, at] = x_high
        x_parts[layer, 1, :, at] = x_low
        queries, key_rows, value_rows = (
            dot3(p_qkv[layer, 0, :, part * WIDTH:(part + 1) * WIDTH], p_qkv[layer, 1, :, part * WIDTH:(part + 1) * WIDTH],
                 x_high, x_low, left_t=True)
            for part in range(3))
        yield
        q_high, q_low = split((queries + col(layer, V_Q)) * QUERY_SCALE)
        k_high, k_low = split(key_rows)
        v_high, v_low = split(value_rows + col(layer, V_V))
        for head in range(HEADS):
            rows = slice(head * HEAD, (head + 1) * HEAD)
            q_all[layer, head, 0:64, at] = q_high[rows]
            q_all[layer, head, 64:128, at] = q_high[rows]
            q_all[layer, head, 128:192, at] = q_low[rows]
            k_all[layer, head, 0:64, at] = k_high[rows]
            k_all[layer, head, 64:128, at] = k_low[rows]
            k_all[layer, head, 128:192, at] = k_high[rows]
            v_all[layer, head, 0:64, at] = v_high[rows]
            v_all[layer, head, 64:128, at] = v_low[rows]
            v_all[layer, head, 128:192, at] = v_high[rows]

    def project(layer, blocks):
        skewed(project_block(layer, block) for block in blocks)

    def attend(layer):
        def two_heads(pair, inside):
            def one_block(index):
                head = pair * 2 + index // BLOCKS
                rows = span(head * HEAD, HEAD)
                at = block_at(index % BLOCKS)
                scores = dot(k_all[layer, head], q_all[layer, head, :, at], left_t=True)
                yield
                top = jnp.max(scores, axis=0, keepdims=True)
                weights = jnp.exp2(scores - top)
                total = jnp.sum(weights, axis=0, keepdims=True)
                high, low = split(weights)
                both = dot(v_all[layer, head, 0:128, :], high)
                context = both[:64] + both[64:] + dot(v_all[layer, head, 0:64, :], low)
                context = context / total
                ctx_parts[layer, 0, rows, at], ctx_parts[layer, 1, rows, at] = split(context)
                log_total = top + jnp.log(total) * LOG2E
                q_all[layer, head, 192:208, at] = feature_tile(marks[:, at], -log_total, 4)

            skewed(one_block(index) for index in range(2 * BLOCKS))
            return inside

        lax.fori_loop(0, HEADS // 2, two_heads, 0)

    def feed_block(layer, block):
        at = block_at(block)
        upper = x_now[:, at] + dot3(
            p_out[layer, 0], p_out[layer, 1], ctx_parts[layer, 0, :, at], ctx_parts[layer, 1, :, at], left_t=True
        ) + col(layer, V_OUT)
        normed, inverse = norm_rows(upper)
        n_one[layer, :, at] = normed
        r_one[layer, :, at] = inverse
        hidden = normed * col(layer, V_GAIN1) + col(layer, V_SHIFT1)
        hid_high, hid_low = split(hidden)
        yield
        in_bias = jnp.concatenate([col(layer, V_IN), col(layer, V_IN + 1)], axis=0)
        pre = dot3(p_in[layer, 0], p_in[layer, 1], hid_high, hid_low, left_t=True) + in_bias
        share = 0.5 + 0.5 * lax.erf(pre * math.sqrt(0.5))
        slope[layer, :, at] = share + pre * (jnp.exp(pre * pre * -0.5) * (1.0 / math.sqrt(2.0 * math.pi)))
        inner_high, inner_low = split(pre * share)
        inner_parts[layer, 0, :, at] = inner_high
        inner_parts[layer, 1, :, at] = inner_low
        yield
        lower = hidden + dot3(p_back[layer, 0], p_back[layer, 1], inner_high, inner_low, left_t=True) + col(layer, V_BACK)
        normed, inverse = norm_rows(lower)
        n_two[layer, :, at] = normed
        r_two[layer, :, at] = inverse
        x_now[:, at] = live[0:1, at] * (normed * col(layer, V_GAIN2) + col(layer, V_SHIFT2))

    def feed_forward(layer):
        skewed(feed_block(layer, block) for block in range(BLOCKS))

    for copy in w_owns:
        copy.wait()
    for copy in w_sends:
        copy.wait()
    load_weights(0)
    x_own.wait()
    x_now[:, :HALF] = x_in[0].T
    project(0, (0, 1))
    load_weights(1)
    for part in range(2):
        x_sends[part].wait()
        if part == 1:
            for copy in c_sends:
                copy.start()
        x_now[:, block_at(2 + part)] = x_in[1, part * BLOCK:(part + 1) * BLOCK].T
        project(0, (2 + part,))
    attend(0)
    feed_forward(0)
    project(1, (0, 1, 2, 3))
    attend(1)
    feed_forward(1)

    x_in[0] = x_now[:, :HALF].T
    x_in[1] = x_now[:, HALF:].T
    y_send = remote(x_in.at[1], final_ref.at[half], torus.partner)
    y_own = pltpu.make_async_copy(x_in.at[0], final_ref.at[half], local_sem.at[7])
    for copy in c_owns + c_sends:
        copy.wait()
    y_send.start()
    y_own.start()
    for part in range(2):
        x_now[part * 128:(part + 1) * 128, :HALF] = far[part].T
        x_now[part * 128:(part + 1) * 128, HALF:] = far[2 + part].T

    bufs = {
        "grads": grads, "cores": cores, "slots": (slots_0, slots_1, slots_2),
        "partial": (partial_0, partial_1), "done": done, "far": far,
    }

    def unit_sum(number, layer, first, count, order):
        return UnitSum(torus, remote, bufs, total_ref, out_sem.at[number], layer, first, count, order)

    dp_parts = dqkv.at[:, 0:INNER]
    hid_parts = dqkv.at[:, INNER:INNER + WIDTH]

    def add_sum(index, values):
        sums[index] += lane_fold(values)

    def back_block(layer, block):
        at = block_at(block)
        grad = live[0:1, at] * x_now[:, at]
        normed = n_two[layer, :, at]
        add_sum(V_GAIN2, grad * normed)
        add_sum(V_SHIFT2, grad)
        d_lower = norm_back(grad * col(layer, V_GAIN2), normed, r_two[layer, :, at])
        add_sum(V_BACK, d_lower)
        high, low = split(d_lower)
        dl_parts[0, :, at] = high
        dl_parts[1, :, at] = low
        yield
        d_pre = dot3(p_back[layer, 0], p_back[layer, 1], high, low) * slope[layer, :, at]
        add_sum(V_IN, d_pre[:WIDTH])
        add_sum(V_IN + 1, d_pre[WIDTH:])
        high, low = split(d_pre)
        dp_parts[0, :, at] = high
        dp_parts[1, :, at] = low
        yield
        d_hidden = d_lower + dot3(p_in[layer, 0], p_in[layer, 1], high, low)
        normed = n_one[layer, :, at]
        hid_parts[0, :, at], hid_parts[1, :, at] = split(normed * col(layer, V_GAIN1) + col(layer, V_SHIFT1))
        add_sum(V_GAIN1, d_hidden * normed)
        add_sum(V_SHIFT1, d_hidden)
        d_upper = norm_back(d_hidden * col(layer, V_GAIN1), normed, r_one[layer, :, at])
        add_sum(V_OUT, d_upper)
        x_now[:, at] = d_upper
        high, low = split(d_upper)
        du_parts[0, :, at] = high
        du_parts[1, :, at] = low
        yield
        d_context = dot3(p_out[layer, 0], p_out[layer, 1], high, low)
        high, low = split(d_context)
        context = ctx_parts[layer, 0, :, at].astype(F32) + ctx_parts[layer, 1, :, at].astype(F32)
        product = d_context * context
        for head in range(HEADS):
            rows = slice(head * HEAD, (head + 1) * HEAD)
            do_all[head, 0:64, at] = high[rows]
            do_all[head, 64:128, at] = high[rows]
            do_all[head, 128:192, at] = low[rows]
            row_dot = jnp.sum(product[rows], axis=0, keepdims=True)
            do_all[head, 192:208, at] = feature_tile(jnp.zeros((16, BLOCK), F32), -row_dot, 0)

    def finish_back(layer, blocks):
        skewed(back_block(layer, block) for block in blocks)

    def put(layer, unit, first, values):
        rows = values.shape[0]
        for part in range(values.shape[1] // 128):
            begin = first + part * rows
            grads[layer, unit, begin:begin + rows, :] = values[:, part * 128:(part + 1) * 128]

    def finish_grads(layer):
        put(layer, 0, 0, dot3(
            inner_parts[layer, 0], inner_parts[layer, 1], dl_parts[0], dl_parts[1], right_t=True))
        put(layer, 1, 0, dot3(hid_parts[0], hid_parts[1], dp_parts[0], dp_parts[1], right_t=True))
        grad_out = dot3(ctx_parts[layer, 0], ctx_parts[layer, 1], du_parts[0], du_parts[1], right_t=True)
        put(layer, 2, 0, grad_out[:, :128])
        put(layer, 3, 0, grad_out[:, 128:])

    def attend_back(layer, after_head):
        def one_head(head, inside):
            rows = span(head * HEAD, HEAD)
            products, parts = {}, {}

            def scores(block):
                at = block_at(block)
                products[block] = (
                    dot(q_all[layer, head, :, at], k_all[layer, head], left_t=True),
                    dot(do_all[head, :, at], v_all[layer, head], left_t=True),
                )

            def weigh(block):
                exponent, d_probs = products.pop(block)
                probs = jnp.exp2(exponent)
                parts[block] = split(probs) + split(probs * d_probs)

            def multiply(block):
                at = block_at(block)
                p_high, p_low, s_high, s_low = parts.pop(block)
                both = dot(k_all[layer, head, 0:128, :], s_high, right_t=True)
                d_query = (both[:64] + both[64:] + dot(k_all[layer, head, 0:64, :], s_low, right_t=True)) * KEY_SCALE
                sums[V_Q, rows, :] += lane_fold(d_query)
                dqkv[0, rows, at], dqkv[1, rows, at] = split(d_query)
                both = dot(q_all[layer, head, 64:192, at], s_high)
                d_key = both[:64] + both[64:] + dot(q_all[layer, head, 64:128, at], s_low)
                both = dot(do_all[head, 64:192, at], p_high)
                d_value = both[:64] + both[64:] + dot(do_all[head, 64:128, at], p_low)
                if block > 0:
                    d_key = dkv[0:64, :] + d_key
                    d_value = dkv[64:128, :] + d_value
                if block < BLOCKS - 1:
                    dkv[0:64, :] = d_key
                    dkv[64:128, :] = d_value
                    return
                k_rows = span(WIDTH + head * HEAD, HEAD)
                v_rows = span(2 * WIDTH + head * HEAD, HEAD)
                dqkv[0, k_rows, :], dqkv[1, k_rows, :] = split(d_key * LN2)
                dqkv[0, v_rows, :], dqkv[1, v_rows, :] = split(d_value)
                sums[V_V, rows, :] += lane_fold(d_value)

            staged(BLOCKS, scores, weigh, multiply)
            for number, todo in enumerate(after_head):

                @pl.when(head == number)
                def _():
                    todo()

            return inside

        lax.fori_loop(0, HEADS, one_head, 0)

    def project_back(layer):
        for block in range(BLOCKS):
            at = block_at(block)
            total = x_now[:, at]
            for part in range(3):
                rows = slice(part * WIDTH, (part + 1) * WIDTH)
                total = total + dot3(
                    p_qkv[layer, 0, :, rows], p_qkv[layer, 1, :, rows], dqkv[0, rows, at], dqkv[1, rows, at])
            x_now[:, at] = total

    def project_grads(layer, pair):
        for part in range(3):
            rows = slice(part * WIDTH + pair * 128, part * WIDTH + (pair + 1) * 128)
            begin = WIDTH + part * WIDTH
            grads[layer, 2 + pair, begin:begin + WIDTH, :] = dot3(
                x_parts[layer, 0], x_parts[layer, 1], dqkv[0, rows], dqkv[1, rows], right_t=True)

    def sum_lanes(layer):
        lane_small = lax.broadcasted_iota(jnp.int32, (WIDTH, 128), 1)
        packed = jnp.zeros((WIDTH, 128), F32)
        for index in range(10):
            packed = jnp.where(lane_small == index, jnp.sum(sums[index], axis=1, keepdims=True), packed)
        small[layer] = packed.T[:SMALL_ROWS]

    def steps(*sums_of):
        def run():
            for one in sums_of:
                one.step()
        return run

    one_a = unit_sum(0, 1, 0, 2, "yzx")
    one_b = unit_sum(1, 1, 2, 2, "zyx")
    zero_a = unit_sum(2, 0, 0, 2, "zyx")
    zero_b = unit_sum(3, 0, 2, 1, "xyz")
    zero_c = unit_sum(4, 0, 3, 1, "yzx")

    def nothing():
        pass

    sums[...] = jnp.zeros_like(sums)
    finish_back(1, range(BLOCKS))
    finish_grads(1)
    one_a.step()
    attend_back(1, [one_a.step, nothing, one_a.step])
    project_grads(1, 0)
    project_grads(1, 1)
    one_b.step()
    one_a.step()
    project_back(1)
    sum_lanes(1)

    sums[...] = jnp.zeros_like(sums)
    one_b.step()
    one_a.step()
    finish_back(0, range(BLOCKS))
    one_a.step()
    finish_grads(0)
    zero_a.step()
    one_b.step()
    one_a.step()

    def after_second():
        one_b.step()
        project_grads(0, 0)
        zero_b.step()

    attend_back(0, [
        zero_a.step, after_second, steps(one_a, zero_a, one_b, zero_b), steps(one_a, zero_a, one_b),
    ])
    project_grads(0, 1)
    zero_c.step()
    sum_lanes(0)
    small_copy = remote(small.at[1 - core], small_far, torus.sibling)
    small_copy.start()
    project_back(0)
    y_own.wait()
    y_send.wait()
    x_in[1] = x_now[:, HALF:].T
    d_send = remote(x_in.at[1], grad_ref.at[half], torus.partner)
    d_send.start()
    zero_c.step()
    x_in[0] = x_now[:, :HALF].T
    d_own = pltpu.make_async_copy(x_in.at[0], grad_ref.at[half], local_sem.at[8])
    d_own.start()
    small_copy.wait()
    small_now = small[core] + small_far[...]
    rounds = ((zero_b, one_b), (zero_b, zero_a), (zero_b, zero_a, one_b), (zero_b, zero_a), (zero_b, zero_a))
    for number, others in enumerate(rounds):
        copies = []
        if number < 3:
            axis = "yzx"[number]
            place = small_slots.at[number, torus.axes[axis][0]]
            place[...] = small_now
            copies = [remote(place, place, device) for _, device in torus.peers(axis)]
            for copy in copies:
                copy.start()
        zero_c.step()
        for one in others:
            one.step()
        for copy in copies:
            copy.wait()
        if number < 3:
            small_now = (small_slots[number, 0] + small_slots[number, 1]) + (
                small_slots[number, 2] + small_slots[number, 3])
    small_ref[...] = small_now
    for one in (one_b, zero_a, zero_b, zero_b, zero_c, zero_c):
        one.step()
    d_own.wait()
    d_send.wait()
    assert all(one.next == 9 for one in (one_a, one_b, zero_a, zero_b, zero_c))


def relay(*operands):
    anywhere = pl.BlockSpec(memory_space=pl.ANY)
    vmem = pl.BlockSpec(memory_space=pltpu.VMEM)
    shape = jax.ShapeDtypeStruct
    f32 = lambda *dims: pltpu.VMEM(dims, F32)
    bf16 = lambda *dims: pltpu.VMEM(dims, BF16)
    copies = 4 + 5 + 2 + 5 * (1 + 9 + 9 + 1) + 1 + 9
    return pl.pallas_call(
        relay_kernel,
        out_shape=(
            shape((2, HALF, WIDTH), F32),
            shape((2, HALF, WIDTH), F32),
            shape((UNITS, UNIT_ROWS, 128), F32),
            shape((SMALL_ROWS, WIDTH), F32),
        ),
        in_specs=[anywhere] * 7 + [vmem] * 8,
        out_specs=(anywhere, anywhere, anywhere, vmem),
        scratch_shapes=[
            f32(2, HALF, WIDTH), pltpu.SMEM((3, 1, 4), jnp.int32),
            f32(2, SMALL_ROWS, WIDTH),
            bf16(2, 2, WIDTH, 3 * WIDTH), bf16(2, 2, WIDTH, WIDTH), bf16(2, 2, WIDTH, INNER), bf16(2, 2, INNER, WIDTH),
            f32(2, WIDTH, 128),
            f32(16, SLOT), f32(8, SLOT), f32(WIDTH, SLOT), bf16(2, 2, WIDTH, SLOT),
            bf16(2, HEADS, DEEP, SLOT), bf16(2, HEADS, DEEP, SLOT), bf16(2, HEADS, DEEP, SLOT),
            bf16(2, 2, WIDTH, SLOT),
            f32(2, WIDTH, SLOT), f32(2, 1, SLOT), f32(2, INNER, SLOT), bf16(2, 2, INNER, SLOT),
            f32(2, WIDTH, SLOT), f32(2, 1, SLOT),
            bf16(2, WIDTH, SLOT), bf16(2, WIDTH, SLOT),
            bf16(HEADS, DEEP, SLOT), f32(2 * HEAD, SLOT), bf16(2, 3 * WIDTH, SLOT), f32(10, WIDTH, 128),
            f32(2, UNITS, UNIT_ROWS, 128), f32(2, UNITS, UNIT_HALF, 128),
            f32(3, 2, UNITS, CHUNKS[0], 128), f32(3, 2, UNITS, CHUNKS[1], 128), f32(3, 2, UNITS, CHUNKS[2], 128),
            f32(2, UNITS, CHUNKS[0], 128), f32(2, UNITS, CHUNKS[1], 128),
            f32(2, UNITS, UNIT_HALF, 128), f32(UNITS, UNIT_HALF, 128),
            f32(2, SMALL_ROWS, WIDTH), f32(SMALL_ROWS, WIDTH), f32(3, 4, SMALL_ROWS, WIDTH),
            pltpu.SemaphoreType.DMA((11,)),
            pltpu.SemaphoreType.DMA((5, 2)),
            pltpu.SemaphoreType.DMA((copies,)),
            pltpu.SemaphoreType.DMA((copies,)),
        ],
        compiler_params=pltpu.CompilerParams(
            collective_id=0, has_side_effects=True, vmem_limit_bytes=VMEM_BYTES),
        name="relay",
    )(*operands)


def unpack_kernel(
    final_in, grad_in, total_in, small_in,
    final_out, grad_out, w_qkv, b_qv, w_out, b_out, gain_one, shift_one, w_in, b_in, w_back, b_back, gain_two, shift_two,
    final_now, grad_now, total_now, in_sem, sem,
):
    arrivals = [
        pltpu.make_async_copy(src, dst, in_sem.at[i])
        for i, (src, dst) in enumerate(((final_in, final_now), (grad_in, grad_now), (total_in, total_now)))
    ]
    for copy in arrivals:
        copy.start()

    def block(unit, first, rows):
        return total_now.at[unit, pl.ds(first, rows)]

    def lanes(ref, part):
        return ref.at[0, :, pl.ds(part * 128, 128)]

    pairs = [(block(0, 512 * part, 512), lanes(w_back, part)) for part in range(2)]
    pairs += [(block(1, 256 * part, 256), lanes(w_in, part)) for part in range(4)]
    pairs += [(block(2 + part, 0, 256), lanes(w_out, part)) for part in range(2)]
    pairs += [(block(2 + part % 2, 256 + 256 * (part // 2), 256), lanes(w_qkv, part)) for part in range(6)]
    copies = []

    def send(src, dst):
        copy = pltpu.make_async_copy(src, dst, sem.at[len(copies)])
        copy.start()
        copies.append(copy)

    for ref, first, count in (
        (b_qv, V_Q, 2), (b_out, V_OUT, 1), (gain_one, V_GAIN1, 1), (shift_one, V_SHIFT1, 1), (b_in, V_IN, 2),
        (b_back, V_BACK, 1), (gain_two, V_GAIN2, 1), (shift_two, V_SHIFT2, 1),
    ):
        for part in range(count):
            ref[:, part * WIDTH:(part + 1) * WIDTH] = small_in[first + part:first + part + 1, :]
    arrivals[0].wait()
    send(final_now, final_out)
    arrivals[1].wait()
    send(grad_now, grad_out)
    arrivals[2].wait()
    for src, dst in pairs:
        send(src, dst)
    for copy in copies:
        copy.wait()


def unpack(final_output, input_grad, total, small):
    anywhere = pl.BlockSpec(memory_space=pl.ANY)
    vmem = pl.BlockSpec(memory_space=pltpu.VMEM)
    shapes = [
        (2, HALF, WIDTH), (2, HALF, WIDTH), (1, WIDTH, 3 * WIDTH), (1, 2 * WIDTH), (1, WIDTH, WIDTH), (1, WIDTH),
        (1, WIDTH), (1, WIDTH), (1, WIDTH, INNER), (1, INNER), (1, INNER, WIDTH), (1, WIDTH), (1, WIDTH), (1, WIDTH),
    ]
    return pl.pallas_call(
        unpack_kernel,
        out_shape=tuple(jax.ShapeDtypeStruct(dims, F32) for dims in shapes),
        in_specs=[anywhere, anywhere, anywhere, vmem],
        out_specs=tuple(anywhere if len(dims) == 3 else vmem for dims in shapes),
        scratch_shapes=[
            pltpu.VMEM((2, HALF, WIDTH), F32), pltpu.VMEM((2, HALF, WIDTH), F32), pltpu.VMEM((UNITS, UNIT_ROWS, 128), F32),
            pltpu.SemaphoreType.DMA((3,)), pltpu.SemaphoreType.DMA((16,)),
        ],
        compiler_params=pltpu.CompilerParams(vmem_limit_bytes=VMEM_BYTES),
        name="unpack",
    )(final_output, input_grad, total, small)


def body(
    activations, cotangent, cell_lengths, w_qkv, b_qv, w_out, b_out, gain_one, shift_one,
    w_in, b_in, w_back, b_back, gain_two, shift_two,
):
    return unpack(*relay(
        activations, cotangent, jnp.transpose(cell_lengths, (2, 1, 0)), w_qkv, w_out, w_in, w_back,
        b_qv, b_out, gain_one, shift_one, b_in, b_back, gain_two, shift_two))


def solution(mesh):
    rows = P(None, ("dp", "seq"), None)
    matrix = P("pipe", None, None)
    vector = P("pipe", None)
    in_specs = (
        rows, rows, P(None, "dp", None), matrix, vector, matrix, vector, vector, vector,
        matrix, vector, matrix, vector, vector, vector,
    )
    out_rows = P("pipe", ("dp", "seq"), None)
    out_specs = (
        out_rows, out_rows, matrix, vector, matrix, vector, vector, vector,
        matrix, vector, matrix, vector, vector, vector,
    )
    return jax.shard_map(body, mesh=mesh, in_specs=in_specs, out_specs=out_specs, check_vma=False)
```

profile of v0, /device:TPU:0, one launch (start us, length us, event | category | flops | bytes accessed | tf_op | source)
XLA Modules:
  0.0 151.6 jit_solution(11250464506283251124)
XLA Ops:
  0.7 145.6 %relay.1 = (f32[2,512,256]{2,1,0:T(8,128)}, f32[2,512,256]{2,1,0:T(8,128)}, f32[4,1024,128]{2,1,0:T(8,128)}, f32[16,256]{1,0:T(8,128)}) custom-call(f32[4,512,256]{2,1,0:T(8,128)} %act_ref.1, f32[4,512,256]{2,1,0:T(8,128)} %cot_ref.1, s32[3,1,4]{2,1,0:T(1,128)} %bitcast.1, f32[1,256,768]{2,1,0:T(8,128)} %w_qkv_ref.1, f32[1,256,256]{2,1,0:T(8,128)} %w_out_ref.1, ...), custom_call_target="tpu_custom_call" | custom-call | tf_op jit(solution)/shard_map/relay/pallas_call | solution.py:766
  146.3 5.1 %unpack.1 = (f32[2,512,256]{2,1,0:T(8,128)}, f32[2,512,256]{2,1,0:T(8,128)}, f32[1,256,768]{2,1,0:T(8,128)}, f32[1,512]{1,0:T(1,128)}, f32[1,256,256]{2,1,0:T(8,...) custom-call(f32[2,512,256]{2,1,0:T(8,128)} %get-tuple-element.18.fin, ...), custom_call_target="tpu_custom_call" | custom-call | tf_op jit(solution)/shard_map/unpack/pallas_call | solution.py:857
where the time goes:
time: 151 us; the launch traced here: 152 us
  Pallas kernels  151 us (100%)
    pallas_call x1, Pallas kernels, relay(): pl.pallas_call(relay_kernel, out_shape=(shape((2, HALF, WIDTH), F32), sha...  146 us
    pallas_call x1, Pallas kernels, unpack(): pl.pallas_call(unpack_kernel, out_shape=tuple((jax.ShapeDtypeStruct(dims,...  5.07 us

commit v1 on v0

--- a/solution.py
+++ b/solution.py
@@ -28,7 +28,7 @@
 KEY_SCALE = 1.0 / math.sqrt(HEAD)
 
 UNITS, UNIT_ROWS, UNIT_HALF = 4, 1024, 512
-CHUNKS = (128, 32, 8)
+CHUNKS = (128, 32)
 SMALL_ROWS = 16
 VMEM_BYTES = 64 * 2 ** 20 - 2 ** 18
 V_Q, V_V, V_OUT, V_GAIN1, V_SHIFT1, V_IN, V_BACK, V_GAIN2, V_SHIFT2 = 0, 1, 2, 3, 4, 5, 7, 8, 9
@@ -120,7 +120,6 @@
             "z": (z, lambda i: {"dp": x_high * 16 + i * 4 + y}),
         }
 
-        self.far_x = [{"dp": (1 - x_high) * 16 + dp % 16, "seq": i} for i in range(2)]
         self.near = {
             axis: [((index + step) % 4, where((index + step) % 4)) for step in (1, 2, 3)]
             for axis, (index, where) in self.axes.items()
@@ -137,9 +136,9 @@
     def __init__(self, send_sem, recv_sem):
         self.send_sem, self.recv_sem, self.used = send_sem, recv_sem, 0
 
-    def take(self):
-        self.used += 1
-        return self.used - 1
+    def take(self, count=1):
+        self.used += count
+        return self.used - count
 
     def __call__(self, src, dst, device):
         return self.build(self.take(), src, dst, device)
@@ -156,9 +155,9 @@
 
 
 class UnitSum:
-    def __init__(self, torus, remote, bufs, total_ref, local_sems, layer, first, count, order):
+    def __init__(self, torus, remote, bufs, total_ref, done_sem, layer, first, count, order):
         self.torus, self.remote, self.bufs = torus, remote, bufs
-        self.total_ref, self.local_sems = total_ref, local_sems
+        self.total_ref, self.done_sem = total_ref, done_sem
         self.layer, self.units, self.order = layer, slice(first, first + count), order
         self.pending = []
         self.next = 0
@@ -173,11 +172,8 @@
             self.remote.build(index, *maker()).wait()
         self.pending = []
 
-    def offset(self, depth):
-        first = 0
-        for level in range(depth):
-            first = first + self.torus.axes[self.order[level]][0] * CHUNKS[level]
-        return first
+    def place(self, level):
+        return self.torus.axes[self.order[level]][0]
 
     def step(self):
         getattr(self, "step_%d" % self.next)()
@@ -207,8 +203,7 @@
     def gathered(self, level, source):
         size = CHUNKS[level]
         slots = self.bufs["slots"][level]
-        first = self.base(level) + self.torus.axes[self.order[level]][0] * size
-        own = source[self.layer, self.units, span(first, size), :]
+        own = source[self.layer, self.units, span(self.base(level) + self.place(level) * size, size), :]
         return (own + slots[0, self.layer, self.units]) + (
             slots[1, self.layer, self.units] + slots[2, self.layer, self.units])
 
@@ -221,78 +216,80 @@
 
     def step_2(self):
         self.settle()
-        partial = self.bufs["partial"][0]
+        partial = self.bufs["partial"]
         partial[self.layer, self.units] = self.gathered(0, self.bufs["grads"])
         self.scatter(1, partial)
 
+    def spread(self, level, chunk):
+        def maker(step):
+            def make():
+                return chunk(), chunk(), self.torus.peer(self.order[level], step)[1]
+            return make
+
+        self.send([maker(step) for step in (1, 2, 3)])
+
     def step_3(self):
         self.settle()
-        partial = self.bufs["partial"][1]
-        partial[self.layer, self.units] = self.gathered(1, self.bufs["partial"][0])
-        self.scatter(2, partial)
-
-    def spread(self, level):
-        size = CHUNKS[level]
-
-        def maker(step):
-            def make():
-                chunk = self.bufs["done"].at[self.layer, self.units, span(self.offset(level + 1), size)]
-                return chunk, chunk, self.torus.peer(self.order[level], step)[1]
-            return make
-
-        self.send([maker(step) for step in (1, 2, 3)])
+        cross = self.bufs["cross"]
+        cross[self.place(2), self.layer, self.units] = self.gathered(1, self.bufs["partial"])
+        self.spread(2, lambda: cross.at[self.place(2), self.layer, self.units])
 
     def step_4(self):
         self.settle()
-        rows = span(self.offset(3), CHUNKS[2])
-        self.bufs["done"][self.layer, self.units, rows, :] = self.gathered(2, self.bufs["partial"][1])
-        self.spread(2)
+        cross, ring = self.bufs["cross"], self.bufs["ring"]
+        ring[self.layer, self.units, span(self.place(1) * CHUNKS[1], CHUNKS[1]), :] = (
+            cross[0, self.layer, self.units] + cross[1, self.layer, self.units]) + (
+            cross[2, self.layer, self.units] + cross[3, self.layer, self.units])
+        self.spread(1, lambda: ring.at[self.layer, self.units, span(self.place(1) * CHUNKS[1], CHUNKS[1])])
+
+    def rows(self):
+        return span(self.torus.core * UNIT_HALF + self.place(0) * CHUNKS[0], CHUNKS[0])
+
+    def last(self, step, across):
+        device = dict(self.torus.peer(self.order[0], step)[1]) if step else {}
+        if across:
+            device.update(self.torus.sibling)
+        return self.remote.build(
+            self.first_index + step + 4 * across, self.bufs["ring"].at[self.layer, self.units],
+            self.bufs["done"].at[self.units, self.rows()], device)
 
     def step_5(self):
         self.settle()
-        self.spread(1)
-
-    def step_6(self):
-        self.settle()
-        self.spread(0)
-
-    def away_copy(self):
-        return self.remote.build(
-            self.away, self.bufs["done"].at[self.layer, self.units], self.bufs["far"].at[self.units], self.torus.sibling)
-
-    def near_copy(self):
-        return pltpu.make_async_copy(
-            self.bufs["done"].at[self.layer, self.units],
-            self.total_ref.at[self.units, span(self.torus.core * UNIT_HALF, UNIT_HALF)], self.local_sems.at[0])
-
-    def far_copy(self):
-        return pltpu.make_async_copy(
-            self.bufs["far"].at[self.units],
-            self.total_ref.at[self.units, span((1 - self.torus.core) * UNIT_HALF, UNIT_HALF)], self.local_sems.at[1])
-
-    def step_7(self):
-        self.settle()
-        self.away = self.remote.take()
+        self.first_index = self.remote.take(8)
 
         @pl.when(self.torus.core == self.layer)
         def _():
-            self.near_copy().start()
+            for step in (1, 2, 3):
+                self.last(step, 0).start()
+            self.bufs["done"][self.units, self.rows(), :] = self.bufs["ring"][self.layer, self.units]
 
         @pl.when(self.torus.core != self.layer)
         def _():
-            self.away_copy().start()
-
-    def step_8(self):
+            for step in (1, 2, 3, 0):
+                self.last(step, 1).start()
+
+    def copy_out(self):
+        return pltpu.make_async_copy(
+            self.bufs["done"].at[self.units], self.total_ref.at[self.units], self.done_sem)
+
+    def step_6(self):
         @pl.when(self.torus.core == self.layer)
         def _():
-            self.away_copy().wait_recv()
-            self.far_copy().start()
-            self.near_copy().wait()
-            self.far_copy().wait()
+            for step in (1, 2, 3):
+                self.last(step, 0).wait()
+            for step in (0, 1, 2, 3):
+                self.last(step, 1).wait_recv()
+            self.copy_out().start()
 
         @pl.when(self.torus.core != self.layer)
         def _():
-            self.away_copy().wait_send()
+            for step in (1, 2, 3, 0):
+                self.last(step, 1).wait_send()
+
+    def finish(self):
+        @pl.when(self.torus.core == self.layer)
+        def _():
+            self.copy_out().wait()
 
 
 def relay_kernel(
@@ -303,7 +300,7 @@
     marks, live, x_now, x_parts, q_all, k_all, v_all, ctx_parts,
     n_one, r_one, slope, inner_parts, n_two, r_two,
     dl_parts, du_parts, do_all, dkv, dqkv, sums,
-    grads, cores, slots_0, slots_1, slots_2, partial_0, partial_1, done, far, small, small_far, small_slots,
+    grads, cores, slots_0, slots_1, partial, cross, ring, done, small, small_far, small_slots,
     local_sem, out_sem, send_sem, recv_sem,
 ):
     torus = Torus()
@@ -311,13 +308,12 @@
     remote = Sender(send_sem, recv_sem)
 
     barrier = pltpu.get_barrier_semaphore()
-    pl.semaphore_signal(barrier, inc=1, device_id=torus.partner, device_id_type=MESH)
     pl.semaphore_signal(barrier, inc=1, device_id=torus.sibling, device_id_type=MESH)
-    for axis in "yz":
+    for axis in "xyz":
         for _, device in torus.peers(axis):
             pl.semaphore_signal(barrier, inc=1, device_id=device, device_id_type=MESH)
-    pl.semaphore_signal(barrier, inc=1, device_id=torus.far_x[0], device_id_type=MESH)
-    pl.semaphore_signal(barrier, inc=1, device_id=torus.far_x[1], device_id_type=MESH)
+            if axis != "x":
+                pl.semaphore_signal(barrier, inc=1, device_id={**device, **torus.sibling}, device_id_type=MESH)
 
     mine = 2 * core + half
     theirs = 2 * core + 1 - half
@@ -333,7 +329,7 @@
     len_own = pltpu.make_async_copy(len_ref, lengths, local_sem.at[0])
     x_own = pltpu.make_async_copy(act_ref.at[mine], x_in.at[0], local_sem.at[1])
     c_owns = [
-        pltpu.make_async_copy(cot_ref.at[mine, :, pl.ds(part * 128, 128)], far.at[part], local_sem.at[9 + part])
+        pltpu.make_async_copy(cot_ref.at[mine, :, pl.ds(part * 128, 128)], done.at[part, 0:HALF], local_sem.at[9 + part])
         for part in range(2)
     ]
     w_owns = [
@@ -349,14 +345,14 @@
         b_in_ref[:, :WIDTH], b_in_ref[:, WIDTH:], b_back_ref[...], gain_two_ref[...], shift_two_ref[...],
         jnp.zeros((6, WIDTH), F32)], axis=0)
 
-    pl.semaphore_wait(barrier, 10)
+    pl.semaphore_wait(barrier, 16)
 
     x_sends = [
         remote(act_ref.at[theirs, pl.ds(part * BLOCK, BLOCK)], x_in.at[1, pl.ds(part * BLOCK, BLOCK)], torus.partner)
         for part in range(2)
     ]
     c_sends = [
-        remote(cot_ref.at[theirs, :, pl.ds(part * 128, 128)], far.at[2 + part], torus.partner) for part in range(2)
+        remote(cot_ref.at[theirs, :, pl.ds(part * 128, 128)], done.at[2 + part, 0:HALF], torus.partner) for part in range(2)
     ]
     w_sends = [remote(src, dst, torus.sibling) for src, dst in weight_pairs(core)]
     w_sends.append(remote(vecs.at[core], vecs.at[core], torus.sibling))
@@ -515,12 +511,12 @@
     y_send.start()
     y_own.start()
     for part in range(2):
-        x_now[part * 128:(part + 1) * 128, :HALF] = far[part].T
-        x_now[part * 128:(part + 1) * 128, HALF:] = far[2 + part].T
+        x_now[part * 128:(part + 1) * 128, :HALF] = done[part, 0:HALF].T
+        x_now[part * 128:(part + 1) * 128, HALF:] = done[2 + part, 0:HALF].T
 
     bufs = {
-        "grads": grads, "cores": cores, "slots": (slots_0, slots_1, slots_2),
-        "partial": (partial_0, partial_1), "done": done, "far": far,
+        "grads": grads, "cores": cores, "slots": (slots_0, slots_1),
+        "partial": partial, "cross": cross, "ring": ring, "done": done,
     }
 
     def unit_sum(number, layer, first, count, order):
@@ -674,10 +670,10 @@
                 one.step()
         return run
 
-    one_a = unit_sum(0, 1, 0, 2, "yzx")
+    one_a = unit_sum(0, 1, 0, 2, "zyx")
     one_b = unit_sum(1, 1, 2, 2, "zyx")
-    zero_a = unit_sum(2, 0, 0, 2, "zyx")
-    zero_b = unit_sum(3, 0, 2, 1, "xyz")
+    zero_a = unit_sum(2, 0, 0, 2, "yzx")
+    zero_b = unit_sum(3, 0, 2, 1, "zyx")
     zero_c = unit_sum(4, 0, 3, 1, "yzx")
 
     def nothing():
@@ -697,24 +693,22 @@
 
     sums[...] = jnp.zeros_like(sums)
     one_b.step()
-    one_a.step()
     finish_back(0, range(BLOCKS))
     one_a.step()
     finish_grads(0)
     zero_a.step()
-    one_b.step()
-    one_a.step()
 
     def after_second():
-        one_b.step()
         project_grads(0, 0)
         zero_b.step()
 
     attend_back(0, [
-        zero_a.step, after_second, steps(one_a, zero_a, one_b, zero_b), steps(one_a, zero_a, one_b),
+        steps(zero_a, one_b, one_a), after_second, steps(zero_b, zero_a, one_b, one_a), one_b.step,
     ])
     project_grads(0, 1)
     zero_c.step()
+    zero_b.step()
+    zero_a.step()
     sum_lanes(0)
     small_copy = remote(small.at[1 - core], small_far, torus.sibling)
     small_copy.start()
@@ -725,12 +719,13 @@
     d_send = remote(x_in.at[1], grad_ref.at[half], torus.partner)
     d_send.start()
     zero_c.step()
+    one_b.step()
     x_in[0] = x_now[:, :HALF].T
     d_own = pltpu.make_async_copy(x_in.at[0], grad_ref.at[half], local_sem.at[8])
     d_own.start()
     small_copy.wait()
     small_now = small[core] + small_far[...]
-    rounds = ((zero_b, one_b), (zero_b, zero_a), (zero_b, zero_a, one_b), (zero_b, zero_a), (zero_b, zero_a))
+    rounds = ((zero_a, zero_b), (zero_a, zero_b, one_b), (), (zero_b, zero_a), (zero_b,))
     for number, others in enumerate(rounds):
         copies = []
         if number < 3:
@@ -749,11 +744,11 @@
             small_now = (small_slots[number, 0] + small_slots[number, 1]) + (
                 small_slots[number, 2] + small_slots[number, 3])
     small_ref[...] = small_now
-    for one in (one_b, zero_a, zero_b, zero_b, zero_c, zero_c):
-        one.step()
+    for one in (one_a, one_b, zero_a, zero_b, zero_c):
+        one.finish()
     d_own.wait()
     d_send.wait()
-    assert all(one.next == 9 for one in (one_a, one_b, zero_a, zero_b, zero_c))
+    assert all(one.next == 7 for one in (one_a, one_b, zero_a, zero_b, zero_c))
 
 
 def relay(*operands):
@@ -762,7 +757,7 @@
     shape = jax.ShapeDtypeStruct
     f32 = lambda *dims: pltpu.VMEM(dims, F32)
     bf16 = lambda *dims: pltpu.VMEM(dims, BF16)
-    copies = 4 + 5 + 2 + 5 * (1 + 9 + 9 + 1) + 1 + 9
+    copies = 4 + 5 + 2 + 5 * (1 + 12 + 8) + 1 + 9
     return pl.pallas_call(
         relay_kernel,
         out_shape=(
@@ -786,12 +781,12 @@
             bf16(2, WIDTH, SLOT), bf16(2, WIDTH, SLOT),
             bf16(HEADS, DEEP, SLOT), f32(2 * HEAD, SLOT), bf16(2, 3 * WIDTH, SLOT), f32(10, WIDTH, 128),
             f32(2, UNITS, UNIT_ROWS, 128), f32(2, UNITS, UNIT_HALF, 128),
-            f32(3, 2, UNITS, CHUNKS[0], 128), f32(3, 2, UNITS, CHUNKS[1], 128), f32(3, 2, UNITS, CHUNKS[2], 128),
-            f32(2, UNITS, CHUNKS[0], 128), f32(2, UNITS, CHUNKS[1], 128),
-            f32(2, UNITS, UNIT_HALF, 128), f32(UNITS, UNIT_HALF, 128),
+            f32(3, 2, UNITS, CHUNKS[0], 128), f32(3, 2, UNITS, CHUNKS[1], 128),
+            f32(2, UNITS, CHUNKS[0], 128), f32(4, 2, UNITS, CHUNKS[1], 128),
+            f32(2, UNITS, CHUNKS[0], 128), f32(UNITS, UNIT_ROWS, 128),
             f32(2, SMALL_ROWS, WIDTH), f32(SMALL_ROWS, WIDTH), f32(3, 4, SMALL_ROWS, WIDTH),
             pltpu.SemaphoreType.DMA((11,)),
-            pltpu.SemaphoreType.DMA((5, 2)),
+            pltpu.SemaphoreType.DMA((5,)),
             pltpu.SemaphoreType.DMA((copies,)),
             pltpu.SemaphoreType.DMA((copies,)),
         ],
@@ -804,25 +799,15 @@
 def unpack_kernel(
     final_in, grad_in, total_in, small_in,
     final_out, grad_out, w_qkv, b_qv, w_out, b_out, gain_one, shift_one, w_in, b_in, w_back, b_back, gain_two, shift_two,
-    final_now, grad_now, total_now, in_sem, sem,
+    final_now, grad_now, total_now, small_now, wide, narrow, in_sem, sem,
 ):
-    arrivals = [
-        pltpu.make_async_copy(src, dst, in_sem.at[i])
-        for i, (src, dst) in enumerate(((final_in, final_now), (grad_in, grad_now), (total_in, total_now)))
-    ]
+    pairs = [(small_in, small_now)]
+    pairs += [(total_in.at[unit], total_now.at[unit]) for unit in range(UNITS)]
+    pairs += [(final_in.at[part], final_now.at[part]) for part in range(2)]
+    pairs += [(grad_in.at[part], grad_now.at[part]) for part in range(2)]
+    arrivals = [pltpu.make_async_copy(src, dst, in_sem.at[i]) for i, (src, dst) in enumerate(pairs)]
     for copy in arrivals:
         copy.start()
-
-    def block(unit, first, rows):
-        return total_now.at[unit, pl.ds(first, rows)]
-
-    def lanes(ref, part):
-        return ref.at[0, :, pl.ds(part * 128, 128)]
-
-    pairs = [(block(0, 512 * part, 512), lanes(w_back, part)) for part in range(2)]
-    pairs += [(block(1, 256 * part, 256), lanes(w_in, part)) for part in range(4)]
-    pairs += [(block(2 + part, 0, 256), lanes(w_out, part)) for part in range(2)]
-    pairs += [(block(2 + part % 2, 256 + 256 * (part // 2), 256), lanes(w_qkv, part)) for part in range(6)]
     copies = []
 
     def send(src, dst):
@@ -830,26 +815,46 @@
         copy.start()
         copies.append(copy)
 
-    for ref, first, count in (
-        (b_qv, V_Q, 2), (b_out, V_OUT, 1), (gain_one, V_GAIN1, 1), (shift_one, V_SHIFT1, 1), (b_in, V_IN, 2),
-        (b_back, V_BACK, 1), (gain_two, V_GAIN2, 1), (shift_two, V_SHIFT2, 1),
-    ):
-        for part in range(count):
-            ref[:, part * WIDTH:(part + 1) * WIDTH] = small_in[first + part:first + part + 1, :]
+    def block(unit, first, rows):
+        return total_now.at[unit, pl.ds(first, rows)]
+
+    def lanes(ref, part):
+        return ref.at[0, :, pl.ds(part * 128, 128)]
+
     arrivals[0].wait()
-    send(final_now, final_out)
+    for number, (ref, first) in enumerate(((b_qv, V_Q), (b_in, V_IN))):
+        wide[number, :, :WIDTH] = small_now[first:first + 1, :]
+        wide[number, :, WIDTH:] = small_now[first + 1:first + 2, :]
+        send(wide.at[number], ref)
+    for number, (ref, first) in enumerate((
+        (b_out, V_OUT), (gain_one, V_GAIN1), (shift_one, V_SHIFT1), (b_back, V_BACK), (gain_two, V_GAIN2),
+        (shift_two, V_SHIFT2),
+    )):
+        narrow[number] = small_now[first:first + 1, :]
+        send(narrow.at[number], ref)
     arrivals[1].wait()
-    send(grad_now, grad_out)
+    for part in range(2):
+        send(block(0, 512 * part, 512), lanes(w_back, part))
     arrivals[2].wait()
-    for src, dst in pairs:
-        send(src, dst)
+    for part in range(4):
+        send(block(1, 256 * part, 256), lanes(w_in, part))
+    for pair in range(2):
+        arrivals[3 + pair].wait()
+        send(block(2 + pair, 0, 256), lanes(w_out, pair))
+        for part in range(3):
+            send(block(2 + pair, 256 + 256 * part, 256), lanes(w_qkv, 2 * part + pair))
+    for part in range(2):
+        arrivals[5 + part].wait()
+        send(final_now.at[part], final_out.at[part])
+    for part in range(2):
+        arrivals[7 + part].wait()
+        send(grad_now.at[part], grad_out.at[part])
     for copy in copies:
         copy.wait()
 
 
 def unpack(final_output, input_grad, total, small):
     anywhere = pl.BlockSpec(memory_space=pl.ANY)
-    vmem = pl.BlockSpec(memory_space=pltpu.VMEM)
     shapes = [
         (2, HALF, WIDTH), (2, HALF, WIDTH), (1, WIDTH, 3 * WIDTH), (1, 2 * WIDTH), (1, WIDTH, WIDTH), (1, WIDTH),
         (1, WIDTH), (1, WIDTH), (1, WIDTH, INNER), (1, INNER), (1, INNER, WIDTH), (1, WIDTH), (1, WIDTH), (1, WIDTH),
@@ -857,11 +862,12 @@
     return pl.pallas_call(
         unpack_kernel,
         out_shape=tuple(jax.ShapeDtypeStruct(dims, F32) for dims in shapes),
-        in_specs=[anywhere, anywhere, anywhere, vmem],
-        out_specs=tuple(anywhere if len(dims) == 3 else vmem for dims in shapes),
+        in_specs=[anywhere] * 4,
+        out_specs=tuple(anywhere for dims in shapes),
         scratch_shapes=[
             pltpu.VMEM((2, HALF, WIDTH), F32), pltpu.VMEM((2, HALF, WIDTH), F32), pltpu.VMEM((UNITS, UNIT_ROWS, 128), F32),
-            pltpu.SemaphoreType.DMA((3,)), pltpu.SemaphoreType.DMA((16,)),
+            pltpu.VMEM((SMALL_ROWS, WIDTH), F32), pltpu.VMEM((2, 1, INNER), F32), pltpu.VMEM((6, 1, WIDTH), F32),
+            pltpu.SemaphoreType.DMA((9,)), pltpu.SemaphoreType.DMA((26,)),
         ],
         compiler_params=pltpu.CompilerParams(vmem_limit_bytes=VMEM_BYTES),
         name="unpack",

time: 151 us -> 143 us (0.947)
  Pallas kernels: 151 us -> 143 us
    pallas_call x1, Pallas kernels: 146 us -> 139 us  [relay(): pl.pallas_call(relay_kernel, out_shape=(shape((2, HALF, WIDTH), F32), sha...]
where the time goes in v1:
time: 143 us; the launch traced here: 144 us
  Pallas kernels  143 us (100%)
    pallas_call x1, Pallas kernels, relay(): pl.pallas_call(relay_kernel, out_shape=(shape((2, HALF, WIDTH), F32), sha...  139 us
    pallas_call x1, Pallas kernels, unpack(): pl.pallas_call(unpack_kernel, out_shape=tuple((jax.ShapeDtypeStruct(dims,...  3.8 us

profile of v1, /device:TPU:0, one launch (start us, length us, event | category | flops | bytes accessed | tf_op | source)
XLA Modules:
  0.0 143.7 jit_solution(9254571759332387536)
XLA Ops:
  0.7 138.9 %relay.1 = (f32[2,512,256]{2,1,0:T(8,128)}, f32[2,512,256]{2,1,0:T(8,128)}, f32[4,1024,128]{2,1,0:T(8,128)}, f32[16,256]{1,0:T(8,128)}) custom-call(f32[4,512,256]{2,1,0:T(8,128)} %act_ref.1, f32[4,512,256]{2,1,0:T(8,128)} %cot_ref.1, s32[3,1,4]{2,1,0:T(1,128)} %bitcast.1, f32[1,256,768]{2,1,0:T(8,128)} %w_qkv_ref.1, f32[1,256,256]{2,1,0:T(8,128)} %w_out_ref.1, ...), custom_call_target="tpu_custom_call" | custom-call | tf_op jit(solution)/shard_map/relay/pallas_call | solution.py:761
  139.6 3.8 %unpack.1 = (f32[2,512,256]{2,1,0:T(8,128)}, f32[2,512,256]{2,1,0:T(8,128)}, f32[1,256,768]{2,1,0:T(8,128)}, f32[1,512]{1,0:T(1,128)}, f32[1,256,256]{2,1,0:T(8,...) custom-call(f32[2,512,256]{2,1,0:T(8,128)} %get-tuple-element.18.fin, ...), custom_call_target="tpu_custom_call" | custom-call | tf_op jit(solution)/shard_map/unpack/pallas_call | solution.py:862
